TPU v7x, 32 devices: a whole 2x2x4 slice. The times are simulated.
32 devices in a mesh: parts: 2 (over y), dp: 4 (over x, core), fsdp: 4 (over z).
Axes of the slice: x: 2, y: 2, z: 4, core: 2. Of those that a mesh axis runs over, the one named last changes fastest.
Arguments:
- hidden: bfloat16 [16384, 5120], P(('parts', 'dp', 'fsdp')), parts along dimension 0, may hold values from -6 to 6
- queries: bfloat16 [16384, 4096], P(('parts', 'dp', 'fsdp')), parts along dimension 0, may hold values from -180 to 180
- key_matrix: bfloat16 [5120, 512], P('fsdp'), may hold values from -0.078125 to 0.078125
- value_matrix: bfloat16 [5120, 512], P('fsdp'), may hold values from -0.078125 to 0.078125
- key_gain: float32 [128], replicated, may hold values from 0.1 to 1.9
- read_out: float32 [4096], replicated, may hold values from -0.5 to 0.5
- placing: int32 [8, 8], P(('parts', 'fsdp')), parts along dimension 0, may hold values from 0 to 7, as said below
- segments: int32 [16384], P(('parts', 'dp', 'fsdp')), parts along dimension 0, may hold values from 0 to 63, never falling along the last dimension, each value on 1 to 256 neighbouring positions
Outputs:
- head_estimates: float32 [16384, 32], P(('parts', 'dp', 'fsdp')), parts along dimension 0
- estimates: float32 [16384], P(('parts', 'dp', 'fsdp')), parts along dimension 0
There are 2 independent parts, one for each index of `parts`. A program takes and returns all parts, laid end to end along the dimension named above; an argument that names none is the same for every part. Nothing has to cross between parts.
Inputs may be any that keep to these rules, and one draw needn't show every extreme that they name: Each row of placing is a permutation of the packed positions; the 2 blocks of one device always go to 2 different dp ranks (at most 1 block of a device per dp rank). `segments`: segment ids never fall along the tokens; a segment has at most 256 tokens.
All inputs are finite; a program needn't handle non-finite values.
Results may differ from a plain program's by a relative error of at most 0.012.
Values may be sent and summed in bfloat16 or wider, within the bound.
A program may use at most 192 MiB of HBM per device.

v0:
```python
import jax
import jax.numpy as jnp
from jax import lax
from jax.sharding import PartitionSpec as P

QUERY_HEADS = 32
KEY_VALUE_HEADS = 4
HEAD_SIZE = 128
BLK = 256


def rms_keys(raw, gain):
    token_rows = raw.shape[0]
    heads = raw.reshape(token_rows, -1, gain.shape[0])
    scale = lax.rsqrt(jnp.mean(heads * heads, axis=-1, keepdims=True) + 1e-06)
    return (heads * scale * gain).astype(jnp.bfloat16).reshape(token_rows, -1)


def project(source, key_matrix, value_matrix, key_gain):
    key_raw = jnp.dot(
        source,
        lax.all_gather(key_matrix, "fsdp", axis=0, tiled=True),
        preferred_element_type=jnp.float32,
    )
    value_raw = jnp.dot(
        source,
        lax.all_gather(value_matrix, "fsdp", axis=0, tiled=True),
        preferred_element_type=jnp.float32,
    )
    return (rms_keys(key_raw, key_gain), value_raw.astype(jnp.bfloat16))


def attend(query_tile, key_tile, value_tile, tile_s):
    token_rows = query_tile.shape[0]
    head_group = QUERY_HEADS // KEY_VALUE_HEADS
    place = jnp.arange(token_rows, dtype=jnp.int32)
    allowed = (tile_s[:, None] == tile_s[None, :]) & (place[None, :] <= place[:, None])

    def single_group(number):
        query_heads = lax.dynamic_slice_in_dim(
            query_tile, number * head_group * HEAD_SIZE, head_group * HEAD_SIZE, 1
        ).reshape(token_rows, head_group, HEAD_SIZE)
        key_heads = lax.dynamic_slice_in_dim(key_tile, number * HEAD_SIZE, HEAD_SIZE, 1)
        value_heads = lax.dynamic_slice_in_dim(value_tile, number * HEAD_SIZE, HEAD_SIZE, 1)
        scores = jnp.einsum(
            "ard,bd->rab", query_heads, key_heads, preferred_element_type=jnp.float32
        ) / jnp.sqrt(jnp.float32(HEAD_SIZE))
        scores = jnp.where(allowed[None], scores, jnp.float32(-1e30))
        top = jnp.max(scores, axis=-1, keepdims=True)
        expo = jnp.where(allowed[None], jnp.exp(scores - top), jnp.float32(0.0))
        weights = (expo / jnp.sum(expo, axis=-1, keepdims=True)).astype(jnp.bfloat16)
        context = jnp.einsum(
            "rab,bd->ard", weights, value_heads, preferred_element_type=jnp.float32
        )
        return context.reshape(token_rows, head_group * HEAD_SIZE).astype(jnp.bfloat16)

    block_pieces = lax.map(single_group, jnp.arange(KEY_VALUE_HEADS, dtype=jnp.int32))
    return block_pieces.transpose(1, 0, 2).reshape(token_rows, QUERY_HEADS * HEAD_SIZE)


def per_device(hidden, queries, key_matrix, value_matrix, key_gain, read_out, placing, segments):
    groups = lax.axis_size("dp")
    rank_here = lax.axis_index("dp")
    token_rows = hidden.shape[0]
    count = token_rows // BLK
    slots = (count + groups - 1) // groups
    table = placing[0]
    total = table.shape[0]
    numbers = jnp.arange(total, dtype=jnp.int32)
    owner = numbers // count
    within = numbers % count
    target_rank = table // count
    same = (
        (owner[:, None] == owner[None, :])
        & (target_rank[:, None] == target_rank[None, :])
        & (within[None, :] < within[:, None])
    )
    ordinal = jnp.sum(same.astype(jnp.int32), axis=1)
    slot_of = target_rank * slots + ordinal
    home_slot = owner * slots + ordinal
    local_ids = jnp.arange(count, dtype=jnp.int32)
    buffer_ids = jnp.arange(groups * slots, dtype=jnp.int32)
    mine = lax.dynamic_slice_in_dim(slot_of, rank_here * count, count)
    chosen = jnp.sum(jnp.where(mine[None, :] == buffer_ids[:, None], local_ids[None, :], 0), axis=1)
    positions = rank_here * count + local_ids
    sources = jnp.sum(jnp.where(table[None, :] == positions[:, None], numbers[None, :], 0), axis=1)
    arrival = jnp.take(home_slot, sources)
    returning = jnp.sum(
        jnp.where(arrival[None, :] == buffer_ids[:, None], local_ids[None, :], 0), axis=1
    )

    def outgoing(local):
        tiles = local.reshape(count, BLK, local.shape[1])
        return jnp.take(tiles, chosen, axis=0).reshape(groups, slots, BLK, local.shape[1])

    def incoming(arrived):
        flat = arrived.reshape(groups * slots, BLK, arrived.shape[3])
        return jnp.take(flat, arrival, axis=0).reshape(token_rows, arrived.shape[3])

    arrived_q, arrived_h = (
        lax.all_to_all(outgoing(queries), "dp", split_axis=0, concat_axis=0, tiled=True),
        lax.all_to_all(outgoing(hidden), "dp", split_axis=0, concat_axis=0, tiled=True),
    )
    packed_q = incoming(arrived_q)
    packed_k, packed_v = project(incoming(arrived_h), key_matrix, value_matrix, key_gain)
    packed_context = attend(packed_q, packed_k, packed_v, segments)
    context_heads = packed_context.reshape(token_rows, QUERY_HEADS, HEAD_SIZE).astype(jnp.float32)
    head_estimates = jnp.sum(
        context_heads * read_out.reshape(QUERY_HEADS, HEAD_SIZE)[None], axis=-1
    )
    packed_estimates = jnp.sum(head_estimates, axis=1)
    estimate_tiles = packed_estimates.reshape(count, BLK)
    back = jnp.take(estimate_tiles, returning, axis=0).reshape(groups, slots, BLK)
    arrived_e = lax.all_to_all(back, "dp", split_axis=0, concat_axis=0, tiled=True)
    estimates = jnp.take(arrived_e.reshape(groups * slots, BLK), mine, axis=0).reshape(token_rows)
    return (head_estimates, estimates)


def solution(mesh):
    in_specs = (
        P(("parts", "dp", "fsdp"), None),
        P(("parts", "dp", "fsdp"), None),
        P("fsdp", None),
        P("fsdp", None),
        P(),
        P(),
        P(("parts", "fsdp"), None),
        P(("parts", "dp", "fsdp")),
    )
    out_specs = (P(("parts", "dp", "fsdp"), None), P(("parts", "dp", "fsdp")))
    return jax.shard_map(
        per_device, mesh=mesh, in_specs=in_specs, out_specs=out_specs, check_vma=False
    )
```

profile of v0, /device:TPU:17, one launch (start us, length us, event | category | flops | bytes accessed | tf_op | source)
XLA Modules:
  0.0 375.5 jit_solution(15107753571185393128)
XLA Ops:
  7.2 0.7 and_select_fusion.1
  7.8 0.7 fusion.40
  8.7 0.6 compare_and_fusion.1
  9.5 4.0 %fusion.51 = (bf16[2,256,2048]{2,1,0:T(8,128)(2,1)}, bf16[2,256,2048]{2,1,0:T(8,128)(2,1)S(1)}) fusion(bf16[2,256,4096]{2,1,0:T(8,128)(2,1)} %bitcast.126), kind=kLoop, calls=%fused_computation.109 | loop fusion | bytes 8388608 | tf_op jit(solution)/shard_map/jit(_take)/gather | solution.py:94
  13.4 4.3 %gather_fusion.7 = bf16[4,256,2048]{2,1,0:T(8,128)(2,1)} fusion(bf16[2,256,2048]{2,1,0:T(8,128)(2,1)} %get-tuple-element.170, s32[1024]{0:T(1024)S(1)} %pad_clamp_fusion.3), kind=kCustom, calls=%fused_computation.7 | custom fusion | bytes 8388624 | tf_op jit(solution)/shard_map/jit(_take)/gather | solution.py:94
  17.8 2.8 gather_fusion.8
  20.6 7.7 %fusion.33 = bf16[4,1,256,4096]{3,2,1,0:T(8,128)(2,1)} fusion(bf16[4,256,2048]{2,1,0:T(8,128)(2,1)} %gather_fusion.8, bf16[4,256,2048]{2,1,0:T(8,128)(2,1)} %gather_fusion.7, pred[4]{0:T(512)(128)(4,1)S(1)} %compare_and_fusion.2), kind=kLoop, calls=%fused_computation.42 | loop fusion | flops 20971520 | bytes 16777220 | tf_op jit(solution)/shard_map/jit(_take)/select_n | solution.py:94
  28.2 6.2 %all-to-all-start.1 = ((bf16[4,1,256,4096]{3,2,1,0:T(8,128)(2,1)}), bf16[4,1,256,4096]{3,2,1,0:T(8,128)(2,1)}, u32[]{:S(2)}, u32[]{:S(2)}) async-start(bf16[4,1,256,4096]{3,2,1,0:T(8,128)(2,1)} %fusion.33), calls=%async_computation.1 | async-start | bytes 16777216 | tf_op jit(solution)/shard_map/all_to_all | solution.py:101
  34.5 0.7 all-gather.5.cloned.1.call-update
  35.2 4.4 %fusion.50 = (bf16[2,256,2560]{2,1,0:T(8,128)(2,1)}, bf16[2,256,2560]{2,1,0:T(8,128)(2,1)S(1)}) fusion(bf16[2,256,5120]{2,1,0:T(8,128)(2,1)} %bitcast.120), kind=kLoop, calls=%fused_computation.108 | loop fusion | bytes 10485760 | tf_op jit(solution)/shard_map/jit(_take)/gather | solution.py:94
  39.6 4.9 %gather_fusion.3 = bf16[4,256,2560]{2,1,0:T(8,128)(2,1)} fusion(bf16[2,256,2560]{2,1,0:T(8,128)(2,1)} %get-tuple-element.168, s32[1024]{0:T(1024)S(1)} %pad_clamp_fusion.3), kind=kCustom, calls=%fused_computation.3 | custom fusion | bytes 10485776 | tf_op jit(solution)/shard_map/jit(_take)/gather | solution.py:94
  44.5 3.2 gather_fusion.4
  47.7 10.1 %fusion.32 = bf16[4,1,256,5120]{3,2,1,0:T(8,128)(2,1)} fusion(bf16[4,256,2560]{2,1,0:T(8,128)(2,1)} %gather_fusion.4, bf16[4,256,2560]{2,1,0:T(8,128)(2,1)} %gather_fusion.3, pred[4]{0:T(512)(128)(4,1)S(1)} %compare_and_fusion.2), kind=kLoop, calls=%fused_computation.40 | loop fusion | flops 26214400 | bytes 20971524 | tf_op jit(solution)/shard_map/jit(_take)/select_n | solution.py:94
  57.8 69.0 %all-to-all-done.1 = bf16[4,1,256,4096]{3,2,1,0:T(8,128)(2,1)} async-done(((bf16[4,1,256,4096]{3,2,1,0:T(8,128)(2,1)}), bf16[4,1,256,4096]{3,2,1,0:T(8,128)(2,1)}, u32[]{:S(2)}, u32[]{:S(2)}) %all-to-all-start.1) | async-done | bytes 8388640 | tf_op jit(solution)/shard_map/all_to_all | solution.py:101
  126.8 6.8 %all-to-all-start = ((bf16[4,1,256,5120]{3,2,1,0:T(8,128)(2,1)}), bf16[4,1,256,5120]{3,2,1,0:T(8,128)(2,1)}, u32[]{:S(2)}, u32[]{:S(2)}) async-start(bf16[4,1,256,5120]{3,2,1,0:T(8,128)(2,1)} %fusion.32), calls=%async_computation | async-start | bytes 20971520 | tf_op jit(solution)/shard_map/all_to_all | solution.py:102
  133.7 0.7 all-gather.3.cloned.1.call-update
  134.6 0.6 gather_fusion
  135.6 6.1 %fusion.49 = (bf16[4,256,2048]{2,1,0:T(8,128)(2,1)}, bf16[4,256,2048]{2,1,0:T(8,128)(2,1)}) fusion(bf16[4,256,4096]{2,1,0:T(8,128)(2,1)} %bitcast.19), kind=kLoop, calls=%fused_computation.107 | loop fusion | bytes 16777216 | tf_op jit(solution)/shard_map/jit(_take)/gather | solution.py:98
  141.7 2.9 gather_fusion.10
  144.6 4.7 %gather_fusion.9 = bf16[2,256,2048]{2,1,0:T(8,128)(2,1)} fusion(bf16[4,256,2048]{2,1,0:T(8,128)(2,1)} %get-tuple-element.166, s32[1024]{0:T(1024)S(1)} %pad_clamp_fusion.2), kind=kCustom, calls=%fused_computation.9 | custom fusion | bytes 4194312 | tf_op jit(solution)/shard_map/jit(_take)/gather | solution.py:98
  149.3 3.9 %pad_maximum_fusion = bf16[2,256,4096]{2,1,0:T(8,128)(2,1)} fusion(bf16[2,256,2048]{2,1,0:T(8,128)(2,1)S(1)} %gather_fusion.10, bf16[2,256,2048]{2,1,0:T(8,128)(2,1)} %gather_fusion.9), kind=kLoop, calls=%fused_computation.47 | loop fusion | flops 8388608 | bytes 8388608
  153.2 6.5 %copy.35 = bf16[512,4096]{0,1:T(8,128)(2,1)} copy(bf16[512,4096]{1,0:T(8,128)(2,1)} %bitcast.119) | data formatting | bytes 8388608 | tf_op jit(solution)/shard_map/jit(_take)/gather | solution.py:98
  159.7 4.6 %broadcast_select_fusion.1 = bf16[512,4096]{0,1:T(8,128)(2,1)} fusion(bf16[512,4096]{0,1:T(8,128)(2,1)} %copy.35, pred[512]{0:T(512)(128)(4,1)S(1)} %broadcast_in_dim.162), kind=kLoop, calls=%fused_computation.48 | loop fusion | flops 2097152 | bytes 8389120 | tf_op jit(solution)/shard_map/jit(_take)/select_n | solution.py:98
  164.4 84.1 %all-to-all-done = bf16[4,1,256,5120]{3,2,1,0:T(8,128)(2,1)} async-done(((bf16[4,1,256,5120]{3,2,1,0:T(8,128)(2,1)}), bf16[4,1,256,5120]{3,2,1,0:T(8,128)(2,1)}, u32[]{:S(2)}, u32[]{:S(2)}) %all-to-all-start) | async-done | bytes 10485792 | tf_op jit(solution)/shard_map/all_to_all | solution.py:102
  248.5 8.6 %fusion.48 = (bf16[4,256,2560]{2,1,0:T(8,128)(2,1)}, bf16[4,256,2560]{2,1,0:T(8,128)(2,1)}) fusion(bf16[4,256,5120]{2,1,0:T(8,128)(2,1)} %bitcast.8), kind=kLoop, calls=%fused_computation.106 | loop fusion | bytes 20971520 | tf_op jit(solution)/shard_map/jit(_take)/gather | solution.py:98
  257.1 3.2 gather_fusion.5
  260.3 4.7 %gather_fusion.6 = bf16[2,256,2560]{2,1,0:T(8,128)(2,1)} fusion(bf16[4,256,2560]{2,1,0:T(8,128)(2,1)} %get-tuple-element.164, s32[1024]{0:T(1024)S(1)} %pad_clamp_fusion.2), kind=kCustom, calls=%fused_computation.6 | custom fusion | bytes 5242888 | tf_op jit(solution)/shard_map/jit(_take)/gather | solution.py:98
  265.0 8.0 %copy.34 = bf16[512,5120]{1,0:T(8,128)(2,1)} copy(bf16[512,5120]{0,1:T(8,128)(2,1)} %bitcast.121) | data formatting | bytes 10485760 | tf_op jit(solution)/shard_map/dot_general | solution.py:20
  273.3 1.4 copy-done
  275.0 0.5 broadcast_select_fusion
  275.6 1.3 slice-done
  276.9 0.4 slice-done.1
  277.3 2.9 multiply_reduce_fusion.2
  280.3 3.1 bitcast_select_fusion.4
  283.5 6.9 %convolution_convert_fusion = bf16[512,512]{1,0:T(8,128)(2,1)S(1)} fusion(bf16[512,5120]{1,0:T(8,128)(2,1)} %bitcast_select_fusion.4, bf16[5120,512]{1,0:T(8,128)(2,1)} %all-gather.3.cloned.1.call-done), kind=kOutput, calls=%fused_computation.49 | convolution fusion | flops 2684616704 | bytes 11010048 | tf_op jit(solution)/shard_map/dot_general | solution.py:25
  290.4 57.8 %while.13 = (s32[]{:T(128)}, bf16[4,512,1024]{1,2,0:T(8,128)(2,1)}, s32[4]{0:T(128)S(1)}, bf16[512,512]{1,0:T(8,128)(2,1)S(1)}, bf16[512,512]{0,1:T(8,128)(2,1)S...) while((s32[]{:T(128)}, bf16[4,512,1024]{1,2,0:T(8,128)(2,1)}, ...), condition=%wide.region_7.8_spmd.clone, body=%wide.region_4.7_spmd.clone.sunk | while | flops 1089733120 | bytes 24152816 | solution.py:57
  290.7 0.6 dynamic_slice.62
  291.9 1.3 constant_dynamic-slice_fusion.2
  294.1 5.8 %fusion.68 = (f32[8,512]{1,0:T(8,128)S(1)}, f32[8,512,512]{1,2,0:T(8,128)}) fusion(pred[512,512]{0,1:T(8,128)(4,1)S(1)} %fusion.67, bf16[512,8,128]{0,2,1:T(8,128)(2,1)S(1)} %bitcast.117, bf16[512,512]{0,1:T(8,128)(2,1)S(1)} %get-tuple-element.255, s32[]{:T(128)S(6)} %select_n.348), kind=kOutput, calls=%fused_computation.105.clone.1 | convolution fusion | flops 547357184 | bytes 10108932 | tf_op jit(solution)/shard_map/while/body/eval_jaxpr/sub | solution.py:50
  299.8 4.2 %fusion.69 = bf16[128,8,512]{2,0,1:T(8,128)(2,1)S(1)} fusion(f32[8,512,512]{1,2,0:T(8,128)} %get-tuple-element.223, f32[8,512]{1,0:T(8,128)S(1)} %get-tuple-element.224, bf16[512,512]{1,0:T(8,128)(2,1)S(1)} %get-tuple-element.254, s32[]{:T(128)S(6)} %select_n.348), kind=kOutput, calls=%fused_computation.21.clone.1 | convolution fusion | flops 541589504 | bytes 9584644 | tf_op jit(solution)/shard_map/while/body/eval_jaxpr/rab,bd->ard/dot_general | solution.py:52
  304.0 1.1 constant_dynamic-update-slice_fusion.4
  305.1 0.6 dynamic_slice.62
  306.3 1.3 constant_dynamic-slice_fusion.2
  308.5 5.8 %fusion.68 = (f32[8,512]{1,0:T(8,128)S(1)}, f32[8,512,512]{1,2,0:T(8,128)}) fusion(pred[512,512]{0,1:T(8,128)(4,1)S(1)} %fusion.67, bf16[512,8,128]{0,2,1:T(8,128)(2,1)S(1)} %bitcast.117, bf16[512,512]{0,1:T(8,128)(2,1)S(1)} %get-tuple-element.255, s32[]{:T(128)S(6)} %select_n.348), kind=kOutput, calls=%fused_computation.105.clone.1 | convolution fusion | flops 547357184 | bytes 10108932 | tf_op jit(solution)/shard_map/while/body/eval_jaxpr/sub | solution.py:50
  314.2 4.2 %fusion.69 = bf16[128,8,512]{2,0,1:T(8,128)(2,1)S(1)} fusion(f32[8,512,512]{1,2,0:T(8,128)} %get-tuple-element.223, f32[8,512]{1,0:T(8,128)S(1)} %get-tuple-element.224, bf16[512,512]{1,0:T(8,128)(2,1)S(1)} %get-tuple-element.254, s32[]{:T(128)S(6)} %select_n.348), kind=kOutput, calls=%fused_computation.21.clone.1 | convolution fusion | flops 541589504 | bytes 9584644 | tf_op jit(solution)/shard_map/while/body/eval_jaxpr/rab,bd->ard/dot_general | solution.py:52
  318.4 1.1 constant_dynamic-update-slice_fusion.4
  319.5 0.6 dynamic_slice.62
  320.7 1.3 constant_dynamic-slice_fusion.2
  322.9 5.7 %fusion.68 = (f32[8,512]{1,0:T(8,128)S(1)}, f32[8,512,512]{1,2,0:T(8,128)}) fusion(pred[512,512]{0,1:T(8,128)(4,1)S(1)} %fusion.67, bf16[512,8,128]{0,2,1:T(8,128)(2,1)S(1)} %bitcast.117, bf16[512,512]{0,1:T(8,128)(2,1)S(1)} %get-tuple-element.255, s32[]{:T(128)S(6)} %select_n.348), kind=kOutput, calls=%fused_computation.105.clone.1 | convolution fusion | flops 547357184 | bytes 10108932 | tf_op jit(solution)/shard_map/while/body/eval_jaxpr/sub | solution.py:50
  328.6 4.1 %fusion.69 = bf16[128,8,512]{2,0,1:T(8,128)(2,1)S(1)} fusion(f32[8,512,512]{1,2,0:T(8,128)} %get-tuple-element.223, f32[8,512]{1,0:T(8,128)S(1)} %get-tuple-element.224, bf16[512,512]{1,0:T(8,128)(2,1)S(1)} %get-tuple-element.254, s32[]{:T(128)S(6)} %select_n.348), kind=kOutput, calls=%fused_computation.21.clone.1 | convolution fusion | flops 541589504 | bytes 9584644 | tf_op jit(solution)/shard_map/while/body/eval_jaxpr/rab,bd->ard/dot_general | solution.py:52
  332.8 1.0 constant_dynamic-update-slice_fusion.4
  333.8 0.6 dynamic_slice.62
  335.0 1.3 constant_dynamic-slice_fusion.2
  337.2 5.7 %fusion.68 = (f32[8,512]{1,0:T(8,128)S(1)}, f32[8,512,512]{1,2,0:T(8,128)}) fusion(pred[512,512]{0,1:T(8,128)(4,1)S(1)} %fusion.67, bf16[512,8,128]{0,2,1:T(8,128)(2,1)S(1)} %bitcast.117, bf16[512,512]{0,1:T(8,128)(2,1)S(1)} %get-tuple-element.255, s32[]{:T(128)S(6)} %select_n.348), kind=kOutput, calls=%fused_computation.105.clone.1 | convolution fusion | flops 547357184 | bytes 10108932 | tf_op jit(solution)/shard_map/while/body/eval_jaxpr/sub | solution.py:50
  343.0 4.1 %fusion.69 = bf16[128,8,512]{2,0,1:T(8,128)(2,1)S(1)} fusion(f32[8,512,512]{1,2,0:T(8,128)} %get-tuple-element.223, f32[8,512]{1,0:T(8,128)S(1)} %get-tuple-element.224, bf16[512,512]{1,0:T(8,128)(2,1)S(1)} %get-tuple-element.254, s32[]{:T(128)S(6)} %select_n.348), kind=kOutput, calls=%fused_computation.21.clone.1 | convolution fusion | flops 541589504 | bytes 9584644 | tf_op jit(solution)/shard_map/while/body/eval_jaxpr/rab,bd->ard/dot_general | solution.py:52
  347.1 1.1 constant_dynamic-update-slice_fusion.4
  348.2 6.6 %convert_element_type.55 = f32[4,512,1024]{1,2,0:T(8,128)} convert(bf16[4,512,1024]{1,2,0:T(8,128)(2,1)} %get-tuple-element.91) | non-fusion elementwise | flops 2097152 | bytes 12582912 | tf_op jit(solution)/shard_map/convert_element_type | solution.py:107
  354.8 2.7 multiply_reduce_fusion
  357.6 0.6 gather_fusion.1
  358.2 0.6 copy.38
  358.8 4.0 %all-to-all-start.2 = ((f32[4,1,256]{2,1,0:T(1,128)}), f32[4,1,256]{2,1,0:T(1,128)S(1)}, u32[]{:S(2)}, u32[]{:S(2)}) async-start(f32[4,1,256]{2,1,0:T(1,128)} %copy.38), calls=%async_computation.2 | async-start | bytes 8192 | tf_op jit(solution)/shard_map/all_to_all | solution.py:114
  362.8 4.6 %multiply_reduce_fusion.1 = f32[512,32]{0,1:T(8,128)} fusion(f32[512,32,128]{0,2,1:T(8,128)} %bitcast.116, f32[32,128]{1,0:T(8,128)S(1)} %bitcast.129), kind=kLoop, calls=%fused_computation.44 | loop fusion | flops 4177920 | bytes 8470528 | tf_op jit(solution)/shard_map/reduce_sum | solution.py:108
  367.4 0.6 gather_fusion.2
  368.0 0.6 copy.44
  (56 shorter events, 2.6 us)
Async XLA Ops:
  28.2 98.6 %all-to-all-start.1 = ((bf16[4,1,256,4096]{3,2,1,0:T(8,128)(2,1)}), bf16[4,1,256,4096]{3,2,1,0:T(8,128)(2,1)}, u32[]{:S(2)}, u32[]{:S(2)}) async-start(bf16[4,1,256,4096]{3,2,1,0:T(8,128)(2,1)} %fusion.33), calls=%async_computation.1 | async-start | bytes 16777216 | tf_op jit(solution)/shard_map/all_to_all | solution.py:101
  34.5 230.5 %all-gather.5.cloned.1.call-start = ((), (), s32[]{:S(2)}) async-start(), calls=%async_computation.4 | async-start | bytes 6553600 | tf_op jit(solution)/shard_map/all_gather | solution.py:22
  57.8 76.6 %copy-start.5 = (s32[1,8]{1,0:T(1,128)S(1)}, s32[1,8]{1,0:T(1,128)}, u32[]{:S(2)}) copy-start(s32[1,8]{1,0:T(1,128)} %param.16) | copy-start | bytes 100
  57.8 77.6 %copy-start.2 = (f32[4096]{0:T(1024)S(1)}, f32[4096]{0:T(1024)}, u32[]{:S(2)}) copy-start(f32[4096]{0:T(1024)} %param.15) | copy-start | bytes 49156
  126.8 121.7 %all-to-all-start = ((bf16[4,1,256,5120]{3,2,1,0:T(8,128)(2,1)}), bf16[4,1,256,5120]{3,2,1,0:T(8,128)(2,1)}, u32[]{:S(2)}, u32[]{:S(2)}) async-start(bf16[4,1,256,5120]{3,2,1,0:T(8,128)(2,1)} %fusion.32), calls=%async_computation | async-start | bytes 20971520 | tf_op jit(solution)/shard_map/all_to_all | solution.py:102
  133.7 149.8 %all-gather.3.cloned.1.call-start = ((), (), s32[]{:S(2)}) async-start(), calls=%async_computation.3 | async-start | bytes 6553600 | tf_op jit(solution)/shard_map/all_gather | solution.py:27
  273.0 1.7 copy-start
  274.7 2.2 slice-start
  275.0 2.2 slice-start.1
  277.3 2.9 copy-start.4
  283.5 7.0 %copy-start.1 = (s32[512]{0:T(512)S(1)}, s32[512]{0:T(512)}, u32[]{:S(2)}) copy-start(s32[512]{0:T(512)} %param.17) | copy-start | bytes 6148
  357.5 10.4 %copy-start.3 = (pred[2]{0:T(512)(128)(4,1)S(1)}, pred[2]{0:T(512)(128)(4,1)}, u32[]{:S(2)}) copy-start(pred[2]{0:T(512)(128)(4,1)} %get-tuple-element.158) | copy-start | bytes 10
  358.8 8.6 %all-to-all-start.2 = ((f32[4,1,256]{2,1,0:T(1,128)}), f32[4,1,256]{2,1,0:T(1,128)S(1)}, u32[]{:S(2)}, u32[]{:S(2)}) async-start(f32[4,1,256]{2,1,0:T(1,128)} %copy.38), calls=%async_computation.2 | async-start | bytes 8192 | tf_op jit(solution)/shard_map/all_to_all | solution.py:114
Sparse Core Ops, SparseCore 0:
  36.9 97.3 all-gather.4
  136.0 97.3 all-gather.2
where the time goes:
time: 377 us; the launch traced here: 375 us
  waiting for transfers between devices  155 us (41%)
  local copies, waits for them, and re-layouts  86.9 us (23%)
  matrix products  49.4 us (13%)
  other arithmetic  47.6 us (13%)
  starting transfers between devices  17.1 us (5%)
  between operations  14.2 us (4%)
  loops' own time  5.55 us (1%)
    all_to_all x1, waiting for transfers between devices, per_device(): lax.all_to_all(outgoing(hidden), 'dp', split_axis=0, concat_axis=0, tiled...  84.1 us
    all_to_all x1, waiting for transfers between devices, per_device(): lax.all_to_all(outgoing(queries), 'dp', split_axis=0, concat_axis=0, tile...  69 us
    gather x7, local copies, waits for them, and re-layouts, incoming(): return jnp.take(flat, arrival, axis=0).reshape(token_rows, arrived.shape[3])  36.7 us
    gather x6, local copies, waits for them, and re-layouts, outgoing(): jnp.take(tiles, chosen, axis=0).reshape(groups, slots, BLK, local.shape[1])  23.6 us
    sub x4, matrix products, single_group(): expo = jnp.where(allowed[None], jnp.exp(scores - top), jnp.float32(0.0))  23 us
    select_n x3, other arithmetic, outgoing(): jnp.take(tiles, chosen, axis=0).reshape(groups, slots, BLK, local.shape[1])  17.8 us
    dot_general x4, matrix products, single_group(): jnp.einsum('rab,bd->ard', weights, value_heads, preferred_element_type=jn...  16.6 us
    select_n x4, other arithmetic, incoming(): return jnp.take(flat, arrival, axis=0).reshape(token_rows, arrived.shape[3])  8.34 us
  transfers between devices with their start and end apart: 5, of which 2 were waited for; matrix products, arithmetic and copies ran while one was open for 24% of the time, Pallas kernels for 0%

commit v1 on v0

v1 whole, which is shorter than its diff:
```python
import math

import jax
import jax.numpy as jnp
from jax import lax
from jax.experimental import pallas as pl
from jax.experimental.pallas import tpu as pltpu
from jax.sharding import PartitionSpec as P

QUERY_HEADS = 32
KEY_VALUE_HEADS = 4
HEAD_SIZE = 128
BLK = 256
GROUP = QUERY_HEADS // KEY_VALUE_HEADS
KEY_WIDTH = KEY_VALUE_HEADS * HEAD_SIZE
NEG = -1e30


def attend_kernel(idx_ref, q_ref, kp_ref, ko_ref, scol_ref, srow_ref, out_ref):
    place_a = lax.broadcasted_iota(jnp.int32, (BLK, BLK), 0)
    place_b = lax.broadcasted_iota(jnp.int32, (BLK, BLK), 1)
    column = scol_ref[0]
    row = srow_ref[0]
    bias_p = jnp.where(column == row[:, :BLK], 0.0, NEG)
    bias_o = jnp.where((column == row[:, BLK:]) & (place_b <= place_a), 0.0, NEG)
    bias = jnp.concatenate([bias_p, bias_o], axis=1)
    lane = lax.broadcasted_iota(jnp.int32, (BLK, HEAD_SIZE), 1)
    both = 2 * BLK
    readout = jnp.concatenate([kp_ref[0, :, KEY_WIDTH:], ko_ref[0, :, KEY_WIDTH:]], axis=0)
    result = jnp.zeros((BLK, HEAD_SIZE), jnp.float32)
    for g in range(KEY_VALUE_HEADS):
        cols = slice(g * HEAD_SIZE, (g + 1) * HEAD_SIZE)
        keys = jnp.concatenate([kp_ref[0, :, cols], ko_ref[0, :, cols]], axis=0)
        for r in range(GROUP):
            h = g * GROUP + r
            q = q_ref[:, h * HEAD_SIZE:(h + 1) * HEAD_SIZE]
            s = lax.dot_general(q, keys, (((1,), (1,)), ((), ())),
                                preferred_element_type=jnp.float32) + bias
            top = jnp.max(s, axis=1, keepdims=True)
            p = jnp.exp2(s - top).astype(jnp.bfloat16)
            o = jnp.dot(p, readout, preferred_element_type=jnp.float32)
            result = jnp.where(lane == h, o / o[:, QUERY_HEADS:QUERY_HEADS + 1], result)
    out_ref[0] = result


def attend(index, queries, keys_all, scol, srow):
    width = keys_all.shape[-1]
    count = scol.shape[0]
    grid_spec = pltpu.PrefetchScalarGridSpec(
        num_scalar_prefetch=1,
        grid=(count,),
        in_specs=[
            pl.BlockSpec((BLK, queries.shape[1]), lambda b, idx: (b, 0)),
            pl.BlockSpec((1, BLK, width), lambda b, idx: (idx[b], 0, 0)),
            pl.BlockSpec((1, BLK, width), lambda b, idx: (idx[count + b], 0, 0)),
            pl.BlockSpec((1, BLK, 1), lambda b, idx: (b, 0, 0)),
            pl.BlockSpec((1, 1, 2 * BLK), lambda b, idx: (b, 0, 0)),
        ],
        out_specs=pl.BlockSpec((1, BLK, HEAD_SIZE), lambda b, idx: (b, 0, 0)),
    )
    return pl.pallas_call(
        attend_kernel,
        grid_spec=grid_spec,
        out_shape=jax.ShapeDtypeStruct((count, BLK, HEAD_SIZE), jnp.float32),
        compiler_params=pltpu.CompilerParams(vmem_limit_bytes=40 * 1024 * 1024),
    )(index, queries, keys_all, keys_all, scol, srow)


def fused_kernel(
    idx_ref, h_hbm, q_hbm, k_ref, v_ref, spread_ref, gain_ref, seg_ref,
    head_ref, est_ref,
    h_buf, q_buf, w_buf, tail_buf, kb0, kb1, kb2, kb3, kb4, seg_buf, bias_buf, res_buf, res_all,
    in_sem, zs, zr, ys, yr, cs, cr, ks, kr, ss, sr, rs, rr,
):
    parts_at = lax.axis_index("parts")
    rank = lax.axis_index("dp")
    z = lax.axis_index("fsdp")
    groups = lax.axis_size("dp")
    n = lax.axis_size("fsdp")
    core = lax.rem(rank, 2)
    sibling = rank + 1 - 2 * core
    other_part = 1 - parts_at
    shard = k_ref.shape[0]
    quarter, half = shard // 4, shard // 2
    kbs = (kb0, kb1, kb2, kb3, kb4)
    chunks = len(kbs)
    count = seg_ref.shape[0]

    def remote(src, dst, send, recv, device):
        return pltpu.make_async_remote_copy(
            src_ref=src, dst_ref=dst, send_sem=send, recv_sem=recv,
            device_id=device, device_id_type=pl.DeviceIdType.MESH)

    load_h = pltpu.make_async_copy(h_hbm, h_buf, in_sem.at[0])
    load_q = pltpu.make_async_copy(q_hbm, q_buf, in_sem.at[1])
    load_h.start()
    load_q.start()

    barrier = pltpu.get_barrier_semaphore()
    peers = [{"parts": parts_at, "dp": rank, "fsdp": lax.rem(z + d, n)} for d in range(1, n)]
    peers += [{"parts": parts_at, "dp": lax.rem(rank + d, groups), "fsdp": z} for d in range(1, groups)]
    peers += [{"parts": other_part, "dp": rank, "fsdp": z}]
    for peer in peers:
        pl.semaphore_signal(barrier, inc=1, device_id=peer, device_id_type=pl.DeviceIdType.MESH)

    high = spread_ref[...].astype(jnp.bfloat16)
    low = (spread_ref[...] - high.astype(jnp.float32)).astype(jnp.bfloat16)
    folded = (jnp.dot(v_ref[...], high, preferred_element_type=jnp.float32)
              + jnp.dot(v_ref[...], low, preferred_element_type=jnp.float32))
    tail_buf[...] = folded.astype(jnp.bfloat16)
    pl.semaphore_wait(barrier, len(peers))

    own_rows = core * half + parts_at * quarter
    peer_rows = core * half + other_part * quarter

    def source(c, first, size):
        if c == 0:
            return tail_buf.at[pl.ds(first, size)]
        return k_ref.at[pl.ds(first, size), pl.ds((c - 1) * HEAD_SIZE, HEAD_SIZE)]

    def behind(d):
        return lax.rem(z - d + n, n)

    def z_copy(c, d):
        return remote(source(c, own_rows, quarter), w_buf.at[c, pl.ds(z * shard + own_rows, quarter)],
                      zs.at[c, d], zr.at[c, d], {"fsdp": lax.rem(z + d, n)})

    def y_copy(c, d):
        at = w_buf.at[c, pl.ds(behind(d) * shard + own_rows, quarter)]
        return remote(at, at, ys.at[c, d], yr.at[c, d], {"parts": other_part})

    def c_copy(c, d):
        at = w_buf.at[c, pl.ds(behind(d) * shard + core * half, half)]
        return remote(at, at, cs.at[c, d], cr.at[c, d], {"dp": sibling})

    def k_copy(c, d):
        at = kbs[c].at[pl.ds(rank * count, count)]
        return remote(at, at, ks.at[c, d], kr.at[c, d], {"dp": lax.rem(rank + d, groups)})

    def s_copy(d):
        return remote(seg_ref, seg_buf.at[pl.ds(rank * count, count)],
                      ss.at[d], sr.at[d], {"dp": lax.rem(rank + d, groups)})

    def r_copy(d):
        at = res_all.at[pl.ds(rank * count, count)]
        return remote(at, at, rs.at[d], rr.at[d], {"dp": lax.rem(rank + d, groups)})

    def start_z(c):
        for d in range(1, n):
            z_copy(c, d).start()

    def pass_y(c):
        for d in range(1, n):
            z_copy(c, d).wait_recv()
            y_copy(c, d).start()

    def pass_core(c):
        for d in range(1, n):
            y_copy(c, d).wait_recv()
            c_copy(c, d).start()

    def project(c):
        for d in range(1, n):
            c_copy(c, d).wait_recv()
        raw = jnp.dot(h_buf[...], w_buf[c], preferred_element_type=jnp.float32)
        if c == 0:
            lane = lax.broadcasted_iota(jnp.int32, raw.shape, 1)
            value = jnp.where(lane == QUERY_HEADS, 1.0, raw)
        else:
            scale = lax.rsqrt(jnp.mean(raw * raw, axis=1, keepdims=True) + 1e-06)
            value = raw * scale * gain_ref[...]
        value = value.astype(jnp.bfloat16)
        for b in range(count):
            kbs[c][rank * count + b] = value[b * BLK:(b + 1) * BLK]
        for d in range(1, groups):
            k_copy(c, d).start()

    def masks():
        for d in range(1, groups):
            s_copy(d).wait_recv()
        place_a = lax.broadcasted_iota(jnp.int32, (BLK, BLK), 0)
        place_b = lax.broadcasted_iota(jnp.int32, (BLK, BLK), 1)
        for b in range(count):
            row = seg_buf[idx_ref[2, b]]
            before = jnp.where(idx_ref[4, b] == 1, seg_buf[idx_ref[3, b]], -1)
            wide = jnp.broadcast_to(row.astype(jnp.float32), (HEAD_SIZE, BLK))
            column = wide.T[:, :1].astype(jnp.int32)
            bias_buf[b, :, :BLK] = jnp.where(column == before, 0.0, NEG)
            bias_buf[b, :, BLK:] = jnp.where((column == row) & (place_b <= place_a), 0.0, NEG)

    def attend_group(c):
        for d in range(1, groups):
            k_copy(c, d).wait_recv()
        lane = lax.broadcasted_iota(jnp.int32, (BLK, HEAD_SIZE), 1)

        def block(b, carry):
            first, second = idx_ref[0, b], idx_ref[1, b]
            readout = jnp.concatenate([kb0[first], kb0[second]], axis=0)
            keys = jnp.concatenate([kbs[c][first], kbs[c][second]], axis=0)
            result = res_buf[b]
            for r in range(GROUP):
                head = (c - 1) * GROUP + r
                q = q_buf[pl.ds(pl.multiple_of(b * BLK, BLK), BLK), head * HEAD_SIZE:(head + 1) * HEAD_SIZE]
                s = lax.dot_general(q, keys, (((1,), (1,)), ((), ())),
                                    preferred_element_type=jnp.float32) + bias_buf[b]
                top = jnp.max(s, axis=1, keepdims=True)
                p = jnp.exp2(s - top).astype(jnp.bfloat16)
                o = jnp.dot(p, readout, preferred_element_type=jnp.float32)
                result = jnp.where(lane == head, o / o[:, QUERY_HEADS:QUERY_HEADS + 1], result)
            res_buf[b] = result
            return carry

        lax.fori_loop(0, count, block, 0)

    start_z(0)
    start_z(1)
    seg_buf[pl.ds(rank * count, count)] = seg_ref[...]
    for d in range(1, groups):
        s_copy(d).start()
    here = pl.multiple_of(z * shard, shard)
    w_buf[0, pl.ds(here, shard)] = tail_buf[...]
    for c in range(1, chunks):
        w_buf[c, pl.ds(here, shard)] = k_ref[:, (c - 1) * HEAD_SIZE:c * HEAD_SIZE]
    res_buf[...] = jnp.zeros_like(res_buf)
    load_h.wait()
    load_q.wait()
    masks()
    for i in range(chunks + 3):
        if i + 2 < chunks:
            start_z(i + 2)
        if i < chunks:
            pass_y(i)
        if 0 <= i - 1 < chunks:
            pass_core(i - 1)
        if 0 <= i - 2 < chunks:
            project(i - 2)
        if i - 3 == 0:
            for d in range(1, groups):
                k_copy(0, d).wait_recv()
        if 1 <= i - 3 < chunks:
            attend_group(i - 3)

    for b in range(count):
        across = res_buf[b].T[:QUERY_HEADS]
        res_all[rank * count + b] = across
        est_ref[b] = jnp.sum(across, axis=0, keepdims=True)
    for d in range(1, groups):
        r_copy(d).start()
    for c in range(chunks):
        for d in range(1, n):
            z_copy(c, d).wait_send()
            y_copy(c, d).wait_send()
            c_copy(c, d).wait_send()
        for d in range(1, groups):
            k_copy(c, d).wait_send()
    for d in range(1, groups):
        s_copy(d).wait_send()
    for d in range(1, groups):
        r_copy(d).wait_recv()
    for b in range(count):
        head_ref[b * BLK:(b + 1) * BLK, :] = res_all[idx_ref[5, b]].T
    for d in range(1, groups):
        r_copy(d).wait_send()


def fused(index, hidden, queries, key_matrix, value_matrix, spread, gain, segments):
    rows, width = hidden.shape
    count = rows // BLK
    n, groups = lax.axis_size("fsdp"), lax.axis_size("dp")
    total = groups * count
    chunks = KEY_VALUE_HEADS + 1
    vmem = pl.BlockSpec(memory_space=pltpu.VMEM)
    anywhere = pl.BlockSpec(memory_space=pl.ANY)
    dma = pltpu.SemaphoreType.DMA
    return pl.pallas_call(
        fused_kernel,
        in_specs=[pl.BlockSpec(memory_space=pltpu.SMEM), anywhere, anywhere, vmem, vmem, vmem, vmem, vmem],
        out_specs=[vmem, vmem],
        out_shape=[
            jax.ShapeDtypeStruct((rows, QUERY_HEADS), jnp.float32),
            jax.ShapeDtypeStruct((count, 1, BLK), jnp.float32),
        ],
        scratch_shapes=[
            pltpu.VMEM((rows, width), jnp.bfloat16),
            pltpu.VMEM(queries.shape, jnp.bfloat16),
            pltpu.VMEM((chunks, width, HEAD_SIZE), jnp.bfloat16),
            pltpu.VMEM((width // n, HEAD_SIZE), jnp.bfloat16),
        ] + [pltpu.VMEM((total, BLK, HEAD_SIZE), jnp.bfloat16)] * chunks + [
            pltpu.VMEM((total, 1, BLK), jnp.int32),
            pltpu.VMEM((count, BLK, 2 * BLK), jnp.float32),
            pltpu.VMEM((count, BLK, HEAD_SIZE), jnp.float32),
            pltpu.VMEM((total, QUERY_HEADS, BLK), jnp.float32),
            dma((2,)),
        ] + [dma((chunks, n))] * 6 + [dma((chunks, groups))] * 2 + [dma((groups,))] * 4,
        compiler_params=pltpu.CompilerParams(
            collective_id=0, has_side_effects=True, vmem_limit_bytes=56 * 1024 * 1024),
        cost_estimate=pl.CostEstimate(flops=10 ** 10, bytes_accessed=2 * 10 ** 7, transcendentals=10 ** 7),
    )(index, hidden, queries, key_matrix, value_matrix, spread, gain, segments)


def per_device(hidden, queries, key_matrix, value_matrix, key_gain, read_out, placing, segments):
    groups = lax.axis_size("dp")
    rank = lax.axis_index("dp")
    rows = hidden.shape[0]
    count = rows // BLK
    total = groups * count
    table = placing[0]
    numbers = jnp.arange(total, dtype=jnp.int32)
    source = jnp.sum(jnp.where(table[None, :] == numbers[:, None], numbers[None, :], 0), axis=1)
    own = rank * count + jnp.arange(count, dtype=jnp.int32)
    packed = jnp.take(table, own)
    odd = (packed % 2) == 1
    partner = jnp.where(odd, jnp.take(source, jnp.maximum(packed - 1, 0)), own)
    head = jnp.arange(QUERY_HEADS)
    spread = jnp.where(
        (head[None, None, :] // GROUP) == jnp.arange(KEY_VALUE_HEADS)[:, None, None],
        read_out.reshape(QUERY_HEADS, HEAD_SIZE).T[None],
        0.0,
    ).reshape(KEY_WIDTH, QUERY_HEADS)
    gain = key_gain * jnp.float32(math.log2(math.e) / math.sqrt(HEAD_SIZE))
    kept = lax.dynamic_slice_in_dim(source, rank * count, count)
    before = jnp.maximum(packed - 1, 0)

    if lax.axis_size("parts") == 2 and groups % 2 == 0 and key_matrix.shape[0] % 64 == 0:
        index = jnp.stack([partner, own, packed, before, odd, kept]).astype(jnp.int32)
        wide = jnp.pad(spread, ((0, 0), (0, HEAD_SIZE - QUERY_HEADS)))
        head_estimates, estimates = fused(
            index, hidden, queries, key_matrix, value_matrix, wide,
            gain.reshape(1, HEAD_SIZE), segments.reshape(count, 1, BLK))
        return (head_estimates, estimates.reshape(rows))

    seg_all = lax.all_gather(segments, "dp", axis=0, tiled=True).reshape(total, BLK)
    seg_own = jnp.take(seg_all, packed, axis=0)
    seg_partner = jnp.take(seg_all, before, axis=0)
    seg_partner = jnp.where(odd[:, None], seg_partner, -1)
    srow = jnp.concatenate([seg_partner, seg_own], axis=1).reshape(count, 1, 2 * BLK)
    scol = seg_own.reshape(count, BLK, 1)

    folded = jnp.dot(value_matrix.astype(jnp.float32), spread, precision=lax.Precision.HIGHEST)
    folded = jnp.pad(folded.astype(jnp.bfloat16), ((0, 0), (0, HEAD_SIZE - QUERY_HEADS)))
    weights = jnp.concatenate([key_matrix, folded], axis=1)
    weights = lax.all_gather(weights, "fsdp", axis=0, tiled=True)
    raw = jnp.dot(hidden, weights, preferred_element_type=jnp.float32)
    heads = raw[:, :KEY_WIDTH].reshape(rows, KEY_VALUE_HEADS, HEAD_SIZE)
    scale = lax.rsqrt(jnp.mean(heads * heads, axis=-1, keepdims=True) + 1e-06)
    keys = (heads * scale * gain).astype(jnp.bfloat16).reshape(rows, KEY_WIDTH)
    lane = jnp.arange(HEAD_SIZE)
    tail = jnp.where(lane[None, :] == QUERY_HEADS, 1.0, raw[:, KEY_WIDTH:]).astype(jnp.bfloat16)
    mine = jnp.concatenate([keys, tail], axis=1)
    everyone = lax.all_gather(mine, "dp", axis=0, tiled=True).reshape(total, BLK, -1)
    index = jnp.concatenate([partner, own]).astype(jnp.int32)
    result = attend(index, queries, everyone, scol, srow)[:, :, :QUERY_HEADS]
    estimates = jnp.sum(result, axis=-1).reshape(rows)
    every_result = lax.all_gather(result, "dp", axis=0, tiled=True)
    head_estimates = jnp.take(every_result, kept, axis=0)
    return (head_estimates.reshape(rows, QUERY_HEADS), estimates)


def solution(mesh):
    in_specs = (
        P(("parts", "dp", "fsdp"), None),
        P(("parts", "dp", "fsdp"), None),
        P("fsdp", None),
        P("fsdp", None),
        P(),
        P(),
        P(("parts", "fsdp"), None),
        P(("parts", "dp", "fsdp")),
    )
    out_specs = (P(("parts", "dp", "fsdp"), None), P(("parts", "dp", "fsdp")))
    return jax.shard_map(
        per_device, mesh=mesh, in_specs=in_specs, out_specs=out_specs, check_vma=False
    )
```

time: 377 us -> 92.7 us (0.25)
  waiting for transfers between devices: 155 us -> 0 us
  Pallas kernels: 0 us -> 82.6 us
  local copies, waits for them, and re-layouts: 86.9 us -> 7.01 us
  matrix products: 49.4 us -> 0 us
  other arithmetic: 47.6 us -> 2.09 us
  starting transfers between devices: 17.1 us -> 0 us
  between operations: 14.2 us -> 0.69 us
  loops' own time: 5.55 us -> 0 us
    all_to_all x3 -> x0, waiting for transfers between devices: 153 us -> none  [the longest x1 84.1 us: per_device(): lax.all_to_all(outgoing(hidden), 'dp', split_axis=0, concat_axis=0, tiled...]
    pallas_call x0 -> x1, Pallas kernels: none -> 82.6 us  [fused(): pl.pallas_call(fused_kernel, in_specs=[pl.BlockSpec(memory_space=pltpu.SM...]
    gather x16 -> x2, local copies, waits for them, and re-layouts: 62.1 us -> 1.93 us  [the longest x1 1.29 us: per_device(): packed = jnp.take(table, own)]
    select_n x13 -> x3, other arithmetic: 26.9 us -> 0.03 us  [the longest x1 0.02 us: per_device(): jnp.where(head[None, None, :] // GROUP == jnp.arange(KEY_VALUE_HEADS)[:,...]
    dot_general x6 -> x0, matrix products: 26.4 us -> none  [the longest x4 16.6 us: single_group(): jnp.einsum('rab,bd->ard', weights, value_heads, preferred_element_type=jn...]
    sub x4 -> x0, matrix products: 23 us -> none  [single_group(): expo = jnp.where(allowed[None], jnp.exp(scores - top), jnp.float32(0.0))]
    all_to_all x3 -> x0, starting transfers between devices: 17.1 us -> none  [the longest x1 6.83 us: per_device(): lax.all_to_all(outgoing(hidden), 'dp', split_axis=0, concat_axis=0, tiled...]
    dot_general x1 -> x0, local copies, waits for them, and re-layouts: 7.97 us -> none  [project(): jnp.dot(source, lax.all_gather(key_matrix, 'fsdp', axis=0, tiled=True), p...]
  transfers between devices with their start and end apart: 5 -> 0, of which waited for: 2 -> 0; matrix products, arithmetic and copies ran while one was open for 24% -> 0% of each run, Pallas kernels for 0% -> 0%
where the time goes in v1:
time: 92.7 us; the launch traced here: 92.4 us
  Pallas kernels  82.6 us (89%)
  local copies, waits for them, and re-layouts  7.01 us (8%)
  other arithmetic  2.09 us (2%)
    pallas_call x1, Pallas kernels, fused(): pl.pallas_call(fused_kernel, in_specs=[pl.BlockSpec(memory_space=pltpu.SM...  82.6 us
    unnamed x2, local copies, waits for them, and re-layouts  2.94 us

profile of v1, /device:TPU:17, one launch (start us, length us, event | category | flops | bytes accessed | tf_op | source)
XLA Modules:
  0.0 92.4 jit_solution(8145019358605398421)
XLA Ops:
  0.6 0.8 select_reduce_fusion
  1.4 1.2 %multiply_bitcast_fusion.gain_ref = f32[1,128]{1,0:T(1,128)} fusion(f32[128]{0:T(128)} %param.14), kind=kLoop, calls=%fused_computation.23 | loop fusion | flops 128 | bytes 1024 | tf_op jit(solution)/shard_map/reshape | solution.py:329
  2.6 1.3 %gather_fusion = s32[2]{0:T(128)S(1)} fusion(s32[8]{0:T(128)} %bitcast.19, s32[1024]{0:T(1024)S(1)} %pad_clamp_fusion.1), kind=kCustom, calls=%fused_computation.clone | custom fusion | bytes 24 | tf_op jit(solution)/shard_map/jit(_take)/gather | solution.py:311
  4.0 0.6 gather_fusion.1
  4.6 0.1 fusion.3
  4.7 0.6 stack.28.idx_ref
  5.3 0.8 copy.21
  6.1 0.7 pad.4.spread_ref
  6.8 82.6 %shard_map.95 = (f32[512,32]{1,0:T(8,128)}, f32[2,1,256]{2,1,0:T(1,128)}) custom-call(s32[6,2]{1,0:T(8,128)} %stack.28.idx_ref, bf16[512,5120]{1,0:T(8,128)(2,1)} %h_hbm.1, bf16[512,4096]{1,0:T(8,128)(2,1)} %q_hbm.1, bf16[1280,512]{1,0:T(8,128)(2,1)} %k_ref.1, bf16[1280,512]{1,0:T(8,128)(2,1)} %v_ref.1, f32[512,128]{1,0:T(8,128)} %pad.4.spread_ref, ...), custom_call_target="tpu_custom_call" | custom-call | flops 10000000000 | bytes 20000000 | tf_op jit(solution)/shard_map/pallas_call | solution.py:275
  89.5 1.7 %copy.22 = f32[512,32]{0,1:T(8,128)} copy(f32[512,32]{1,0:T(8,128)} %get-tuple-element.13) | data formatting | bytes 131072
  91.2 1.3 %copy.24 = f32[512]{0:T(512)} copy(f32[512]{0:T(512)} %bitcast.23) | data formatting | bytes 4096
  (9 shorter events, 0.1 us)
